TPU v7x, 32 devices: a whole 2x2x4 slice. The times are simulated.
32 devices in a mesh: groups: 2 (over y), owner: 4 (over z), tp: 2 (over x), rep: 2 (over core).
Axes of the slice: x: 2, y: 2, z: 4, core: 2. Of those that a mesh axis runs over, the one named last changes fastest.
Arguments:
- tokens: bfloat16 [2048, 5120], P(('groups', 'owner', 'rep'), 'tp'), parts along dimension 0, may hold values from -6 to 6
- base_projection_weight: bfloat16 [5120, 5120], P('tp', 'owner'), may hold values from -0.078125 to 0.078125
- adapter_down_weight: bfloat16 [32, 5120, 64], P('owner', 'tp'), may hold values from -0.078125 to 0.078125
- adapter_up_weight: bfloat16 [32, 64, 5120], P('owner', None, 'tp'), may hold values from -0.75 to 0.75
- adapter_output_scale: float32 [32], P('owner'), may hold values from 0.5 to 4
- row_owner_index: int32 [2048, 1], P(('groups', 'owner', 'rep')), parts along dimension 0, may hold values from 0 to 3; in each aligned block of 128 rows (0 to 127, 128 to 255, ...) at most 128 rows name the same one
- row_adapter_slot: int32 [2048], P(('groups', 'owner', 'rep')), parts along dimension 0, may hold values from 0 to 7
Outputs:
- projected: bfloat16 [2048, 5120], P(('groups', 'owner', 'rep'), 'tp'), parts along dimension 0
There are 2 independent parts, one for each index of `groups`. A program takes and returns all parts, laid end to end along the dimension named above; an argument that names none is the same for every part. Nothing has to cross between parts.
Inputs may be any that keep to these rules, and one draw needn't show every extreme that they name: `row_owner_index`: among the rows of one device at most 128 name one owner index, and that bound is reached.
All inputs are finite; a program needn't handle non-finite values.
Results may differ from a plain program's by a relative error of at most 0.0056.
Values may be sent and summed in bfloat16 or wider, within the bound.
A program may use at most 128 MiB of HBM per device.

v0:
```python
import jax
import jax.numpy as jnp
from jax import lax
from jax.sharding import PartitionSpec as P


def local(
    tokens,
    base_projection_weight,
    adapter_down_weight,
    adapter_up_weight,
    adapter_output_scale,
    row_owner_index,
    row_adapter_slot,
):
    row_count = tokens.shape[0]
    local_feature_slice = tokens.shape[1]
    owner_devices = lax.axis_size("owner")
    adapter_slots = row_count * 4 // owner_devices
    local_adapter_output = adapter_down_weight.shape[0]
    adapter_rank_width = adapter_down_weight.shape[2]
    gathered, owners_all, slots_all = (
        lax.all_gather(tokens, "owner", axis=0, tiled=True),
        lax.all_gather(row_owner_index, "owner", axis=0, tiled=True),
        lax.all_gather(row_adapter_slot, "owner", axis=0, tiled=True),
    )
    partial_value = jnp.dot(gathered, base_projection_weight, preferred_element_type=jnp.float32)
    partial_value = partial_value.reshape(owner_devices, row_count, base_projection_weight.shape[1])
    returned = lax.all_to_all(partial_value, "owner", split_axis=0, concat_axis=2, tiled=True)
    full_partial = returned.reshape(row_count, owner_devices * base_projection_weight.shape[1])
    base_output = lax.psum_scatter(full_partial, "tp", scatter_dimension=1, tiled=True)
    owner_ids = row_owner_index[:, 0]
    owner_hot = (owner_ids[:, None] == jnp.arange(owner_devices, dtype=jnp.int32)[None, :]).astype(
        jnp.int32
    )
    before = jnp.cumsum(owner_hot, axis=0) - owner_hot
    row_rank = jnp.sum(before * owner_hot, axis=1)
    position = owner_ids * adapter_slots + row_rank
    dispatch = (
        position[None, :] == jnp.arange(owner_devices * adapter_slots, dtype=jnp.int32)[:, None]
    ).astype(jnp.bfloat16)
    my_index = lax.axis_index("owner")
    mine = (owners_all[:, 0] == my_index).astype(jnp.int32).reshape(owner_devices, row_count)
    earlier = jnp.cumsum(mine, axis=1) - mine
    picker = (
        (earlier[:, None, :] == jnp.arange(adapter_slots, dtype=jnp.int32)[None, :, None])
        & (mine[:, None, :] == 1)
    ).astype(jnp.bfloat16)
    arrived_rows = jnp.einsum(
        "scr,srd->scd",
        picker,
        gathered.reshape(owner_devices, row_count, local_feature_slice),
        preferred_element_type=jnp.float32,
    ).astype(jnp.bfloat16)
    codes = (
        jnp.einsum(
            "scr,sr->sc",
            picker,
            (slots_all + 1).astype(jnp.bfloat16).reshape(owner_devices, row_count),
            preferred_element_type=jnp.float32,
        )
        - 1.0
    )
    arrived_codes = codes.astype(jnp.bfloat16)
    items = arrived_rows.shape[1]
    flattened_rows = arrived_rows.reshape(owner_devices * items, local_feature_slice)
    flat_codes = arrived_codes.reshape(owner_devices * items).astype(jnp.float32)
    select = flat_codes[:, None] == jnp.arange(local_adapter_output, dtype=jnp.float32)[None, :]
    select_f = select.astype(jnp.float32)
    gathered_down_output = jnp.einsum(
        "qe,gej->qgj", flattened_rows, adapter_down_weight, preferred_element_type=jnp.float32
    )
    partial_low = jnp.sum(gathered_down_output * select_f[:, :, None], axis=1)
    summed = lax.psum(partial_low, "tp")
    low_rank = summed.astype(jnp.bfloat16)
    spread = (select.astype(jnp.bfloat16)[:, :, None] * low_rank[:, None, :]).reshape(
        owner_devices * items, local_adapter_output * adapter_rank_width
    )
    expand = jnp.dot(
        spread,
        adapter_up_weight.reshape(local_adapter_output * adapter_rank_width, local_feature_slice),
        preferred_element_type=jnp.float32,
    )
    scale_row = jnp.sum(select_f * adapter_output_scale[None, :], axis=1)
    final_output = (
        (expand * scale_row[:, None])
        .astype(jnp.bfloat16)
        .reshape(owner_devices, items, local_feature_slice)
    )
    returned_adapter_output = lax.all_to_all(
        final_output, "owner", split_axis=0, concat_axis=0, tiled=True
    )
    adapter_input_rows = jnp.dot(
        dispatch.T,
        returned_adapter_output.reshape(owner_devices * adapter_slots, local_feature_slice),
        preferred_element_type=jnp.float32,
    )
    return (base_output + adapter_input_rows).astype(jnp.bfloat16)


def solution(mesh):
    return jax.shard_map(
        local,
        mesh=mesh,
        in_specs=(
            P(("groups", "owner", "rep"), "tp"),
            P("tp", "owner"),
            P("owner", "tp", None),
            P("owner", None, "tp"),
            P("owner"),
            P(("groups", "owner", "rep"), None),
            P(("groups", "owner", "rep")),
        ),
        out_specs=P(("groups", "owner", "rep"), "tp"),
        check_vma=False,
    )
```

profile of v0, /device:TPU:0, one launch (start us, length us, event | category | flops | bytes accessed | tf_op | source)
XLA Modules:
  0.0 249.2 jit_solution(15516360822128214507)
XLA Ops:
  6.5 0.0 copy-start
  6.5 0.0 all-gather.3.cloned.1.call-start
  6.5 0.7 all-gather.3.cloned.1.call-update
  7.3 59.2 %all-gather.3.cloned.1.call-done = bf16[512,2560]{1,0:T(8,128)(2,1)} async-done(((bf16[128,2560]{1,0:T(8,128)(2,1)}), bf16[512,2560]{1,0:T(8,128)(2,1)}) %all-gather.3.cloned.1.call-update) | async-done | bytes 2621456 | tf_op jit(solution)/shard_map/all_gather | solution.py:23
  66.5 8.8 %fusion.24 = f32[512,1280]{1,0:T(8,128)} fusion(bf16[512,2560]{1,0:T(8,128)(2,1)} %all-gather.3.cloned.1.call-done, bf16[2560,1280]{1,0:T(8,128)(2,1)} %param.8), kind=kOutput, calls=%fused_computation.36 | convolution fusion | flops 3355443200 | bytes 11796480 | tf_op jit(solution)/shard_map/dot_general | solution.py:27
  75.2 0.0 copy-start.1
  75.2 0.0 copy-start.2
  75.2 0.0 copy-start.3
  75.2 4.7 %all-to-all-start = ((f32[4,128,1280]{2,1,0:T(8,128)}), f32[4,128,1280]{2,1,0:T(8,128)}, u32[]{:S(2)}, u32[]{:S(2)}) async-start(f32[4,128,1280]{2,1,0:T(8,128)} %bitcast.44), calls=%async_computation | async-start | bytes 5242880 | tf_op jit(solution)/shard_map/all_to_all | solution.py:29
  79.9 0.0 reduce-scatter.2.cloned.1.call-start
  80.0 0.0 copy-done.1
  80.0 48.3 %all_gather.10 = s32[512,1]{0,1:T(1,128)S(1)} all-gather(s32[128,1]{0,1:T(1,128)S(1)} %copy-done.1), channel_id=1, replica_groups=mesh['groups'=2,'owner'=4,'tp'=2,'rep'=2] {'owner'}, dimensions={0}, use_global_device_ids=true | all-gather | bytes 2560 | tf_op jit(solution)/shard_map/all_gather | solution.py:24
  128.3 0.3 reduce_window_sum.23
  128.6 0.0 copy-done.2
  128.6 22.3 %all-gather = s32[4,1,128]{2,1,0:T(1,128)S(1)} all-gather(s32[1,1,128]{2,1,0:T(1,128)S(1)} %bitcast.54), channel_id=1, replica_groups=mesh['groups'=2,'owner'=4,'tp'=2,'rep'=2] {'owner'}, dimensions={0}, use_global_device_ids=true | all-gather | bytes 2560 | tf_op jit(solution)/shard_map/all_gather | solution.py:25
  150.9 0.2 fusion.7
  151.1 0.0 copy-done.3
  151.1 0.1 select_reduce_fusion.1
  151.2 4.1 %convolution_convert_fusion = bf16[4,128,2560]{2,1,0:T(8,128)(2,1)} fusion(bf16[4,128,2560]{2,1,0:T(8,128)(2,1)} %bitcast.43, s32[4,128]{1,0:T(4,128)S(1)} %sub.15, pred[4,128]{1,0:T(4,128)(4,1)S(1)} %broadcast_compare_fusion), kind=kOutput, calls=%fused_computation.2 | convolution fusion | flops 336986112 | bytes 5245440 | tf_op jit(solution)/shard_map/scr,srd->scd/dot_general | solution.py:49
  155.3 0.0 all-to-all-done
  155.3 3.4 %copy.12 = f32[1,128,4,1280]{3,2,1,0:T(4,128)S(1)} copy(f32[1,128,4,1280]{3,1,2,0:T(8,128)} %bitcast.2) | data formatting | bytes 5242880 | tf_op jit(solution)/shard_map/all_to_all | solution.py:29
  158.7 2.0 copy.15
  160.7 0.0 reduce-scatter.2.cloned.1.call-update
  160.7 0.0 copy-done
  160.7 3.3 %fusion.25 = f32[512,512]{0,1:S(1)} fusion(bf16[512,2560]{1,0:T(8,128)(2,1)} %bitcast.45, bf16[2560,512]{0,1:T(8,128)(2,1)S(1)} %bitcast.40), kind=kOutput, calls=%fused_computation.37 | convolution fusion | flops 1342177280 | bytes 6291456
  164.0 0.1 multiply_reduce_fusion
  164.1 12.4 %all-reduce.1 = bf16[512,64]{0,1:T(8,128)(2,1)S(1)} all-reduce(f32[512,64]{0,1:T(8,128)S(1)} %multiply_reduce_fusion), channel_id=1, replica_groups=mesh['groups'=2,'owner'=4,'tp'=2,'rep'=2] {'tp'}, use_global_device_ids=true, to_apply=%region_5.6 | all-reduce | flops 32768 | bytes 196608 | tf_op jit(solution)/shard_map/psum | solution.py:74
  176.6 4.9 %fusion = bf16[512,2560]{1,0:T(8,128)(2,1)} fusion(bf16[8,64,2560]{2,1,0:T(8,128)(2,1)} %param.10, f32[512]{0:T(512)S(1)} %select_reduce_fusion.1, bf16[512,64]{0,1:T(8,128)(2,1)S(1)} %all-reduce.1, bf16[512,8]{0,1:T(8,128)(2,1)S(1)} %get-tuple-element.5), kind=kOutput, calls=%fused_computation.1 | convolution fusion | flops 1345060864 | bytes 5318656 | tf_op jit(solution)/shard_map/dot_general | solution.py:79
  181.5 4.5 %all-to-all-start.1 = ((bf16[4,128,2560]{2,1,0:T(8,128)(2,1)}), bf16[4,128,2560]{2,1,0:T(8,128)(2,1)}, u32[]{:S(2)}, u32[]{:S(2)}) async-start(bf16[4,128,2560]{2,1,0:T(8,128)(2,1)} %bitcast.46), calls=%async_computation.2 | async-start | bytes 5242880 | tf_op jit(solution)/shard_map/all_to_all | solution.py:90
  186.1 0.1 fusion.14
  186.2 0.2 reduce_window_sum.22
  186.3 0.2 select_reduce_fusion
  186.5 52.3 %all-to-all-done.1 = bf16[4,128,2560]{2,1,0:T(8,128)(2,1)} async-done(((bf16[4,128,2560]{2,1,0:T(8,128)(2,1)}), bf16[4,128,2560]{2,1,0:T(8,128)(2,1)}, u32[]{:S(2)}, u32[]{:S(2)}) %all-to-all-start.1) | async-done | bytes 2621472 | tf_op jit(solution)/shard_map/all_to_all | solution.py:90
  238.8 0.0 reduce-scatter.2.cloned.1.call-done
  238.8 3.5 %fusion.1 = bf16[128,2560]{1,0:T(8,128)(2,1)} fusion(f32[128,2560]{1,0:T(8,128)} %reduce-scatter.2.cloned.1.call-done, bf16[512,2560]{1,0:T(8,128)(2,1)} %bitcast.17, s32[128]{0:T(128)S(1)} %multiply_add_fusion), kind=kOutput, calls=%fused_computation.4 | convolution fusion | flops 336265216 | bytes 4588032 | tf_op jit(solution)/shard_map/dot_general | solution.py:93
  (6 shorter events, 0.0 us)
Async XLA Ops:
  6.5 154.2 %copy-start = (bf16[8,2560,64]{1,2,0:T(8,128)(2,1)S(1)}, bf16[8,2560,64]{1,2,0:T(8,128)(2,1)}, u32[]{:S(2)}) copy-start(bf16[8,2560,64]{1,2,0:T(8,128)(2,1)} %param.9) | copy-start | bytes 7864324
  6.5 59.9 %all-gather.3.cloned.1.call-start = ((), (), s32[]{:S(2)}) async-start(), calls=%async_computation.3 | async-start | bytes 3276800 | tf_op jit(solution)/shard_map/all_gather | solution.py:23
  75.2 4.7 %copy-start.1 = (s32[128,1]{0,1:T(1,128)S(1)}, s32[128,1]{0,1:T(1,128)}, u32[]{:S(2)}) copy-start(s32[128,1]{0,1:T(1,128)} %param.12) | copy-start | bytes 1540
  75.2 53.4 %copy-start.2 = (s32[128]{0:T(128)S(1)}, s32[128]{0:T(128)}, u32[]{:S(2)}) copy-start(s32[128]{0:T(128)} %param.13) | copy-start | bytes 1540
  75.2 75.8 %copy-start.3 = (f32[8]{0:T(128)S(1)}, f32[8]{0:T(128)}, u32[]{:S(2)}) copy-start(f32[8]{0:T(128)} %param.11) | copy-start | bytes 100
  75.2 80.1 %all-to-all-start = ((f32[4,128,1280]{2,1,0:T(8,128)}), f32[4,128,1280]{2,1,0:T(8,128)}, u32[]{:S(2)}, u32[]{:S(2)}) async-start(f32[4,128,1280]{2,1,0:T(8,128)} %bitcast.44), calls=%async_computation | async-start | bytes 5242880 | tf_op jit(solution)/shard_map/all_to_all | solution.py:29
  79.9 158.9 %reduce-scatter.2.cloned.1.call-start = ((), (), s32[]{:S(2)}) async-start(), calls=%async_computation.4 | async-start | bytes 3932160 | tf_op jit(solution)/shard_map/reduce_scatter | solution.py:31
  181.5 57.3 %all-to-all-start.1 = ((bf16[4,128,2560]{2,1,0:T(8,128)(2,1)}), bf16[4,128,2560]{2,1,0:T(8,128)(2,1)}, u32[]{:S(2)}, u32[]{:S(2)}) async-start(bf16[4,128,2560]{2,1,0:T(8,128)(2,1)} %bitcast.46), calls=%async_computation.2 | async-start | bytes 5242880 | tf_op jit(solution)/shard_map/all_to_all | solution.py:90
Sparse Core Ops, SparseCore 0:
  8.9 57.4 all-gather.2
  160.8 37.8 reduce-scatter.1
where the time goes:
time: 250 us; the launch traced here: 249 us
  waiting for transfers between devices  112 us (45%)
  blocking collectives  83 us (33%)
  matrix products  24.8 us (10%)
  between operations  13.5 us (5%)
  starting transfers between devices  9.26 us (4%)
  local copies, waits for them, and re-layouts  5.4 us (2%)
    all_gather x1, waiting for transfers between devices, local(): lax.all_gather(tokens, 'owner', axis=0, tiled=True)  59.2 us
    all_to_all x1, waiting for transfers between devices, local(): lax.all_to_all(final_output, 'owner', split_axis=0, concat_axis=0, tiled=...  52.3 us
    all_gather x1, blocking collectives, local(): lax.all_gather(row_owner_index, 'owner', axis=0, tiled=True)  48.3 us
    all_gather x1, blocking collectives, local(): lax.all_gather(row_adapter_slot, 'owner', axis=0, tiled=True)  22.3 us
    psum x1, blocking collectives, local(): summed = lax.psum(partial_low, 'tp')  12.4 us
    dot_general x1, matrix products, local(): jnp.dot(gathered, base_projection_weight, preferred_element_type=jnp.floa...  8.76 us
  transfers between devices with their start and end apart: 4, of which 2 were waited for; matrix products, arithmetic and copies ran while one was open for 5% of the time, Pallas kernels for 0%

commit v1 on v0

--- a/solution.py
+++ b/solution.py
@@ -1,7 +1,16 @@
+import functools
+
 import jax
 import jax.numpy as jnp
 from jax import lax
+from jax.experimental import pallas as pl
+from jax.experimental.pallas import tpu as pltpu
 from jax.sharding import PartitionSpec as P
+
+
+MESH = pl.DeviceIdType.MESH
+CHUNKS = 4
+TILE = 256
 
 
 def local(
@@ -98,9 +107,334 @@
     return (base_output + adapter_input_rows).astype(jnp.bfloat16)
 
 
+def chain_kernel(
+    slots_per_owner,
+    meta_in, scale, tok_hbm, w_hbm, down_hbm, up_hbm, out_ref,
+    tok, w, down, up, meta, arrived, result, base_send, base_recv, base_own, low_own, low_recv,
+    load_sem, tok_send, tok_recv, res_send, res_recv,
+    meta_send, meta_recv, low_ssem, low_rsem, base_ssem, base_rsem,
+):
+    me = lax.axis_index("owner")
+    tp = lax.axis_index("tp")
+    rows = tok.shape[1]
+    width = w.shape[1]
+    features = tok.shape[2]
+    chunk = rows // CHUNKS
+    low_half = me < 2
+    first = (me == 0) | (me == 3)
+    second = jnp.logical_not(first)
+
+    def actual(position):
+        return jnp.where(low_half, position, 3 - position)
+
+    v0, v1, v2 = actual(0), actual(1), actual(2)
+    home = me // (features // width)
+    takes_base = tp == home
+    column = lax.rem(me, features // width) * width
+
+    def part(c):
+        return pl.ds(c * chunk, chunk)
+
+    def remote(src, dst, ssem, rsem, target):
+        return pltpu.make_async_remote_copy(
+            src_ref=src, dst_ref=dst, send_sem=ssem, recv_sem=rsem,
+            device_id={"owner": target}, device_id_type=MESH,
+        )
+
+    def across(src, dst, ssem, rsem):
+        return pltpu.make_async_remote_copy(
+            src_ref=src, dst_ref=dst, send_sem=ssem, recv_sem=rsem,
+            device_id={"tp": 1 - tp}, device_id_type=MESH,
+        )
+
+    def tok_copy(kind, src, dst_slot, c, target):
+        return remote(
+            src.at[part(c)], tok.at[dst_slot, part(c)], tok_send.at[kind, c],
+            tok_recv.at[dst_slot, c], target,
+        )
+
+    def res_copy(slot, dst_slot, c, target):
+        return remote(
+            result.at[slot, part(c)], arrived.at[dst_slot, part(c)], res_send.at[slot, c],
+            res_recv.at[dst_slot, c], target,
+        )
+
+    def meta_copy(k):
+        return remote(
+            meta_in, meta.at[me], meta_send.at[k - 1], meta_recv.at[me], lax.rem(me + k, 4)
+        )
+
+    def meta_arrival(k):
+        source = lax.rem(me + k, 4)
+        return remote(meta_in, meta.at[source], meta_send.at[k - 1], meta_recv.at[source], source)
+
+    def low_copy(slot):
+        return across(low_own.at[slot], low_recv.at[slot], low_ssem.at[slot], low_rsem.at[slot])
+
+    def base_copy(slot):
+        return across(
+            base_send.at[slot], base_recv.at[slot], base_ssem.at[slot], base_rsem.at[slot]
+        )
+
+    loads = [
+        pltpu.make_async_copy(tok_hbm, tok.at[0], load_sem.at[0]),
+        pltpu.make_async_copy(down_hbm, down, load_sem.at[1]),
+        pltpu.make_async_copy(w_hbm, w, load_sem.at[2]),
+        pltpu.make_async_copy(up_hbm, up, load_sem.at[3]),
+    ]
+    barrier = pltpu.get_barrier_semaphore()
+    for k in range(1, 4):
+        pl.semaphore_signal(
+            barrier, inc=1, device_id={"owner": lax.rem(me + k, 4)}, device_id_type=MESH
+        )
+    pl.semaphore_signal(barrier, inc=1, device_id={"tp": 1 - tp}, device_id_type=MESH)
+    for load in loads:
+        load.start()
+    meta[me] = meta_in[...]
+    pl.semaphore_wait(barrier, 4)
+
+    for k in range(1, 4):
+        meta_copy(k).start()
+
+    @pl.when(first)
+    def _():
+        for c in range(CHUNKS):
+            tok_copy(0, tok_hbm, 1, c, v1).start()
+
+    @pl.when(second)
+    def _():
+        for c in range(CHUNKS):
+            tok_copy(0, tok_hbm, 1, c, v0).start()
+            tok_copy(1, tok_hbm, 2, c, v2).start()
+
+    for load in loads:
+        load.wait()
+    for k in range(1, 4):
+        meta_arrival(k).wait_recv()
+
+    lane = lax.broadcasted_iota(jnp.int32, (rows, 128), 1)
+    rank = 64
+    groups = slots_per_owner * rank // 128
+
+    def codes(slot):
+        position = jnp.where(first, slot, jnp.where(slot < 2, 1 - slot, slot))
+        line = meta[actual(position)][0:1, :]
+        return jnp.broadcast_to(line, (128, rows)).T
+
+    def mask_of(code, j):
+        return code == (me * slots_per_owner + (128 // rank) * j + lane // rank).astype(jnp.float32)
+
+    def project(slot):
+        code = codes(slot)
+        x = tok[slot]
+        wide = lax.dot_general(
+            x, down[...], (((1,), (1,)), ((), ())), preferred_element_type=jnp.float32
+        )
+        low = jnp.zeros((rows, 128), jnp.float32)
+        for j in range(groups):
+            low = low + jnp.where(mask_of(code, j), wide[:, 128 * j:128 * (j + 1)], 0.0)
+        low_own[slot] = low
+        low_copy(slot).start()
+
+        @pl.loop(0, width // TILE)
+        def _(n):
+            cols = pl.ds(pl.multiple_of(n * TILE, TILE), TILE)
+            value = jnp.dot(tok[slot], w[:, cols], preferred_element_type=jnp.float32)
+
+            @pl.when(takes_base)
+            def _():
+                base_own[slot, :, cols] = value
+
+            @pl.when(jnp.logical_not(takes_base))
+            def _():
+                base_send[slot, :, cols] = value.astype(jnp.bfloat16)
+
+        @pl.when(jnp.logical_not(takes_base))
+        def _():
+            base_copy(slot).start()
+
+    def finish(slot):
+        code = codes(slot)
+        low_copy(slot).wait_recv()
+        low = low_own[slot] + low_recv[slot]
+        spread = jnp.concatenate(
+            [jnp.where(mask_of(code, j), low, 0.0).astype(jnp.bfloat16) for j in range(groups)],
+            axis=1,
+        )
+        gain = jnp.zeros((rows, 128), jnp.float32)
+        for g in range(slots_per_owner):
+            mine = code == (me * slots_per_owner + g + 0 * lane).astype(jnp.float32)
+            gain = gain + jnp.where(mine, scale[g], 0.0)
+        gain = jnp.concatenate([gain] * (TILE // 128), axis=1)
+
+        @pl.loop(0, features // TILE)
+        def _(n):
+            cols = pl.ds(pl.multiple_of(n * TILE, TILE), TILE)
+            value = jnp.dot(spread, up[:, cols], preferred_element_type=jnp.float32)
+            result[slot, :, cols] = (value * gain).astype(jnp.bfloat16)
+
+        @pl.when(takes_base)
+        def _():
+            base_copy(slot).wait_recv()
+
+            @pl.loop(0, width // TILE)
+            def _(n):
+                here = pl.ds(pl.multiple_of(n * TILE, TILE), TILE)
+                there = pl.ds(pl.multiple_of(column + n * TILE, TILE), TILE)
+                base = base_own[slot, :, here] + base_recv[slot, :, here].astype(jnp.float32)
+                result[slot, :, there] = (
+                    result[slot, :, there].astype(jnp.float32) + base
+                ).astype(jnp.bfloat16)
+
+    @pl.loop(0, 5)
+    def _(step):
+        @pl.when(first & (step >= 1) & (step < 4))
+        def _():
+            for c in range(CHUNKS):
+                tok_copy(0, tok_hbm, step, c, v1).wait_recv()
+
+        @pl.when(second & (step == 1))
+        def _():
+            for c in range(CHUNKS):
+                tok_copy(0, tok_hbm, 1, c, v0).wait_recv()
+                tok_copy(2, tok.at[1], 3, c, v2).start()
+                tok_copy(0, tok_hbm, 2, c, v0).wait_recv()
+                tok_copy(3, tok.at[2], 2, c, v0).start()
+
+        @pl.when(second & (step == 3))
+        def _():
+            for c in range(CHUNKS):
+                tok_copy(0, tok_hbm, 3, c, v0).wait_recv()
+                tok_copy(4, tok.at[3], 3, c, v0).start()
+
+        @pl.when(step < 4)
+        def _():
+            project(step)
+
+        done = jnp.where(first, step, step - 1)
+
+        @pl.when((done >= 0) & (done < 4))
+        def _():
+            finish(done)
+
+        @pl.when(first & (done >= 1) & (done < 4))
+        def _():
+            for c in range(CHUNKS):
+                res_copy(done, done - 1, c, v1).start()
+
+    def add_arrived(slot, source, c):
+        res_copy(slot, source, c, v0).wait_recv()
+        result[slot, part(c)] = (
+            result[slot, part(c)].astype(jnp.float32)
+            + arrived[source, part(c)].astype(jnp.float32)
+        ).astype(jnp.bfloat16)
+
+    @pl.when(second)
+    def _():
+        for slot, source, dst, target in ((2, 1, 3, v2), (3, 2, 4, v2), (1, 4, 0, v0)):
+            for c in range(CHUNKS):
+                add_arrived(slot, source, c)
+                res_copy(slot, dst, c, target).start()
+        for c in range(CHUNKS):
+            add_arrived(0, 3, c)
+
+    for c in range(CHUNKS):
+        res_copy(0, 0, c, v0).wait_recv()
+        out_ref[part(c)] = (
+            result[0, part(c)].astype(jnp.float32) + arrived[0, part(c)].astype(jnp.float32)
+        ).astype(jnp.bfloat16)
+
+    for k in range(1, 4):
+        meta_copy(k).wait_send()
+    for slot in range(4):
+        low_copy(slot).wait_send()
+
+    @pl.when(jnp.logical_not(takes_base))
+    def _():
+        for slot in range(4):
+            base_copy(slot).wait_send()
+
+    for c in range(CHUNKS):
+        tok_copy(0, tok_hbm, 1, c, v0).wait_send()
+        for slot in range(1, 4):
+            res_copy(slot, 0, c, v0).wait_send()
+
+    @pl.when(second)
+    def _():
+        for c in range(CHUNKS):
+            for kind in range(1, 5):
+                tok_copy(kind, tok_hbm, 1, c, v0).wait_send()
+
+
+def fused_local(
+    tokens,
+    base_projection_weight,
+    adapter_down_weight,
+    adapter_up_weight,
+    adapter_output_scale,
+    row_owner_index,
+    row_adapter_slot,
+):
+    rows, features = tokens.shape
+    width = base_projection_weight.shape[1]
+    adapters, _, rank = adapter_down_weight.shape
+    deep = adapters * rank
+    down = jnp.swapaxes(adapter_down_weight, 1, 2).reshape(deep, features)
+    up = adapter_up_weight.reshape(deep, features)
+    code = (row_owner_index[:, 0] * adapters + row_adapter_slot).astype(jnp.float32)
+    meta = jnp.broadcast_to(code[None, :], (8, rows))
+    bf16, f32 = jnp.bfloat16, jnp.float32
+    dma = pltpu.SemaphoreType.DMA
+    vmem = pl.BlockSpec(memory_space=pltpu.VMEM)
+    far = pl.BlockSpec(memory_space=pl.ANY)
+    return pl.pallas_call(
+        functools.partial(chain_kernel, adapters),
+        out_shape=jax.ShapeDtypeStruct((rows, features), bf16),
+        in_specs=[vmem, pl.BlockSpec(memory_space=pltpu.SMEM), far, far, far, far],
+        out_specs=vmem,
+        scratch_shapes=[
+            pltpu.VMEM((4, rows, features), bf16),
+            pltpu.VMEM((features, width), bf16),
+            pltpu.VMEM((deep, features), bf16),
+            pltpu.VMEM((deep, features), bf16),
+            pltpu.VMEM((4, 8, rows), f32),
+            pltpu.VMEM((5, rows, features), bf16),
+            pltpu.VMEM((4, rows, features), bf16),
+            pltpu.VMEM((4, rows, width), bf16),
+            pltpu.VMEM((4, rows, width), bf16),
+            pltpu.VMEM((4, rows, width), f32),
+            pltpu.VMEM((4, rows, 128), f32),
+            pltpu.VMEM((4, rows, 128), f32),
+            dma((4,)),
+            dma((5, CHUNKS)),
+            dma((4, CHUNKS)),
+            dma((4, CHUNKS)),
+            dma((5, CHUNKS)),
+            dma((3,)),
+            dma((4,)),
+            dma((4,)),
+            dma((4,)),
+            dma((4,)),
+            dma((4,)),
+        ],
+        compiler_params=pltpu.CompilerParams(
+            collective_id=0, has_side_effects=True, vmem_limit_bytes=48 * 2**20
+        ),
+        cost_estimate=pl.CostEstimate(
+            flops=8 * rows * features * (width + 2 * deep),
+            bytes_accessed=2 * features * (width + 2 * deep + 2 * rows),
+            transcendentals=0,
+        ),
+    )(meta, adapter_output_scale, tokens, base_projection_weight, down, up)
+
+
+def fits(mesh):
+    return mesh.shape["owner"] == 4 and mesh.shape["tp"] == 2
+
+
 def solution(mesh):
     return jax.shard_map(
-        local,
+        fused_local if fits(mesh) else local,
         mesh=mesh,
         in_specs=(
             P(("groups", "owner", "rep"), "tp"),

time: 250 us -> 96.2 us (0.38)
  waiting for transfers between devices: 112 us -> 0 us
  Pallas kernels: 0 us -> 91 us
  blocking collectives: 83 us -> 0 us
  matrix products: 24.8 us -> 0 us
  between operations: 13.5 us -> 0.01 us
  starting transfers between devices: 9.26 us -> 0 us
    pallas_call x0 -> x1, Pallas kernels: none -> 91 us  [fused_local(): pl.pallas_call(functools.partial(chain_kernel, adapters), out_shape=jax.S...]
    all_gather x2 -> x0, blocking collectives: 70.6 us -> none  [the longest x1 48.3 us: local(): lax.all_gather(row_owner_index, 'owner', axis=0, tiled=True)]
    all_gather x1 -> x0, waiting for transfers between devices: 59.2 us -> none  [local(): lax.all_gather(tokens, 'owner', axis=0, tiled=True)]
    all_to_all x2 -> x0, waiting for transfers between devices: 52.3 us -> none  [the longest x1 52.3 us: local(): lax.all_to_all(final_output, 'owner', split_axis=0, concat_axis=0, tiled=...]
    dot_general x5 -> x0, matrix products: 21.5 us -> none  [the longest x1 8.76 us: local(): jnp.dot(gathered, base_projection_weight, preferred_element_type=jnp.floa...]
    psum x1 -> x0, blocking collectives: 12.4 us -> none  [local(): summed = lax.psum(partial_low, 'tp')]
    all_to_all x2 -> x0, starting transfers between devices: 9.22 us -> none  [the longest x1 4.67 us: local(): lax.all_to_all(partial_value, 'owner', split_axis=0, concat_axis=2, tiled...]
    all_to_all x1 -> x0, local copies, waits for them, and re-layouts: 3.43 us -> none  [local(): lax.all_to_all(partial_value, 'owner', split_axis=0, concat_axis=2, tiled...]
  transfers between devices with their start and end apart: 4 -> 0, of which waited for: 2 -> 0; matrix products, arithmetic and copies ran while one was open for 5% -> 0% of each run, Pallas kernels for 0% -> 0%
where the time goes in v1:
time: 96.2 us; the launch traced here: 96 us
  Pallas kernels  91 us (95%)
  local copies, waits for them, and re-layouts  4.32 us (4%)
    pallas_call x1, Pallas kernels, fused_local(): pl.pallas_call(functools.partial(chain_kernel, adapters), out_shape=jax.S...  91 us
    unnamed x7, local copies, waits for them, and re-layouts  4.32 us

profile of v1, /device:TPU:0, one launch (start us, length us, event | category | flops | bytes accessed | tf_op | source)
XLA Modules:
  0.0 96.0 jit_solution(5521596130004567549)
XLA Ops:
  0.0 0.7 fusion
  0.7 0.0 copy-start
  0.7 1.7 %copy-done = bf16[8,2560,64]{1,2,0:T(8,128)(2,1)S(1)} copy-done((bf16[8,2560,64]{1,2,0:T(8,128)(2,1)S(1)}, bf16[8,2560,64]{1,2,0:T(8,128)(2,1)}, u32[]{:S(2)}) %copy-start) | copy-done | bytes 2621464
  2.4 0.0 copy-start.1
  2.4 1.1 %copy-done.1 = bf16[128,2560]{1,0:T(8,128)(2,1)S(1)} copy-done((bf16[128,2560]{1,0:T(8,128)(2,1)S(1)}, bf16[128,2560]{1,0:T(8,128)(2,1)}, u32[]{:S(2)}) %copy-start.1) | copy-done | bytes 655384
  3.5 0.0 copy-start.2
  3.5 0.7 copy-done.2
  4.2 91.0 %shard_map.73 = bf16[128,2560]{1,0:T(8,128)(2,1)S(1)} custom-call(f32[8,128]{1,0:T(8,128)S(1)} %broadcast_in_dim.2.meta_in, f32[8]{0:T(128)S(1)} %copy-done.2, bf16[128,2560]{1,0:T(8,128)(2,1)S(1)} %copy-done.1, bf16[2560,1280]{1,0:T(8,128)(2,1)} %w_hbm.1, bf16[512,2560]{1,0:T(8,128)(2,1)S(1)} %bitcast.8, bf16[512,2560]{1,0:T(8,128)(2,1)} %bitcast.9), custom_call_target="tpu_custom_call" | custom-call | flops 6039797760 | bytes 13107200 | tf_op jit(solution)/shard_map/pallas_call | solution.py:390
  95.2 0.8 copy.9
  (1 shorter events, 0.0 us)
Async XLA Ops:
  0.7 1.7 %copy-start = (bf16[8,2560,64]{1,2,0:T(8,128)(2,1)S(1)}, bf16[8,2560,64]{1,2,0:T(8,128)(2,1)}, u32[]{:S(2)}) copy-start(bf16[8,2560,64]{1,2,0:T(8,128)(2,1)} %param.9) | copy-start | bytes 7864324
  2.4 1.1 %copy-start.1 = (bf16[128,2560]{1,0:T(8,128)(2,1)S(1)}, bf16[128,2560]{1,0:T(8,128)(2,1)}, u32[]{:S(2)}) copy-start(bf16[128,2560]{1,0:T(8,128)(2,1)} %tok_hbm.1) | copy-start | bytes 1966084
  3.5 0.7 copy-start.2

commit v2 on v1

--- a/solution.py
+++ b/solution.py
@@ -9,7 +9,8 @@
 
 
 MESH = pl.DeviceIdType.MESH
-CHUNKS = 4
+HALVES = 2
+CHUNKS = 8
 TILE = 256
 
 
@@ -110,7 +111,7 @@
 def chain_kernel(
     slots_per_owner,
     meta_in, scale, tok_hbm, w_hbm, down_hbm, up_hbm, out_ref,
-    tok, w, down, up, meta, arrived, result, base_send, base_recv, base_own, low_own, low_recv,
+    tok, w, down, up, meta, arrived, result, base_send, base_recv, base_own, low_own, low_recv, code_of,
     load_sem, tok_send, tok_recv, res_send, res_recv,
     meta_send, meta_recv, low_ssem, low_rsem, base_ssem, base_rsem,
 ):
@@ -120,6 +121,8 @@
     width = w.shape[1]
     features = tok.shape[2]
     chunk = rows // CHUNKS
+    half = rows // HALVES
+    per_half = CHUNKS // HALVES
     low_half = me < 2
     first = (me == 0) | (me == 3)
     second = jnp.logical_not(first)
@@ -133,7 +136,10 @@
     column = lax.rem(me, features // width) * width
 
     def part(c):
-        return pl.ds(c * chunk, chunk)
+        return pl.ds(pl.multiple_of(c * chunk, chunk), chunk)
+
+    def span(h):
+        return pl.ds(pl.multiple_of(h * half, half), half)
 
     def remote(src, dst, ssem, rsem, target):
         return pltpu.make_async_remote_copy(
@@ -149,7 +155,7 @@
 
     def tok_copy(kind, src, dst_slot, c, target):
         return remote(
-            src.at[part(c)], tok.at[dst_slot, part(c)], tok_send.at[kind, c],
+            src.at[span(c)], tok.at[dst_slot, span(c)], tok_send.at[kind, c],
             tok_recv.at[dst_slot, c], target,
         )
 
@@ -168,12 +174,16 @@
         source = lax.rem(me + k, 4)
         return remote(meta_in, meta.at[source], meta_send.at[k - 1], meta_recv.at[source], source)
 
-    def low_copy(slot):
-        return across(low_own.at[slot], low_recv.at[slot], low_ssem.at[slot], low_rsem.at[slot])
-
-    def base_copy(slot):
+    def low_copy(slot, h):
         return across(
-            base_send.at[slot], base_recv.at[slot], base_ssem.at[slot], base_rsem.at[slot]
+            low_own.at[slot, span(h)], low_recv.at[slot, span(h)],
+            low_ssem.at[slot, h], low_rsem.at[slot, h],
+        )
+
+    def base_copy(slot, h):
+        return across(
+            base_send.at[slot, span(h)], base_recv.at[slot, span(h)],
+            base_ssem.at[slot, h], base_rsem.at[slot, h],
         )
 
     loads = [
@@ -198,12 +208,12 @@
 
     @pl.when(first)
     def _():
-        for c in range(CHUNKS):
+        for c in range(HALVES):
             tok_copy(0, tok_hbm, 1, c, v1).start()
 
     @pl.when(second)
     def _():
-        for c in range(CHUNKS):
+        for c in range(HALVES):
             tok_copy(0, tok_hbm, 1, c, v0).start()
             tok_copy(1, tok_hbm, 2, c, v2).start()
 
@@ -212,56 +222,57 @@
     for k in range(1, 4):
         meta_arrival(k).wait_recv()
 
-    lane = lax.broadcasted_iota(jnp.int32, (rows, 128), 1)
     rank = 64
     groups = slots_per_owner * rank // 128
-
-    def codes(slot):
-        position = jnp.where(first, slot, jnp.where(slot < 2, 1 - slot, slot))
+    for slot in range(4):
+        position = jnp.where(first, slot, 1 - slot if slot < 2 else slot)
         line = meta[actual(position)][0:1, :]
-        return jnp.broadcast_to(line, (128, rows)).T
+        code_of[slot] = jnp.broadcast_to(line, (128, rows)).T
+    lane = lax.broadcasted_iota(jnp.int32, (half, 128), 1)
 
     def mask_of(code, j):
         return code == (me * slots_per_owner + (128 // rank) * j + lane // rank).astype(jnp.float32)
 
-    def project(slot):
-        code = codes(slot)
-        x = tok[slot]
+    def project(slot, h):
+        here = span(h)
+        code = code_of[slot, here]
         wide = lax.dot_general(
-            x, down[...], (((1,), (1,)), ((), ())), preferred_element_type=jnp.float32
-        )
-        low = jnp.zeros((rows, 128), jnp.float32)
+            tok[slot, here], down[...], (((1,), (1,)), ((), ())),
+            preferred_element_type=jnp.float32,
+        )
+        low = jnp.zeros((half, 128), jnp.float32)
         for j in range(groups):
             low = low + jnp.where(mask_of(code, j), wide[:, 128 * j:128 * (j + 1)], 0.0)
-        low_own[slot] = low
-        low_copy(slot).start()
+        low_own[slot, here] = low
+        low_copy(slot, h).start()
 
         @pl.loop(0, width // TILE)
         def _(n):
             cols = pl.ds(pl.multiple_of(n * TILE, TILE), TILE)
-            value = jnp.dot(tok[slot], w[:, cols], preferred_element_type=jnp.float32)
+            value = jnp.dot(tok[slot, here], w[:, cols], preferred_element_type=jnp.float32)
 
             @pl.when(takes_base)
             def _():
-                base_own[slot, :, cols] = value
+                base_own[slot, here, cols] = value
 
             @pl.when(jnp.logical_not(takes_base))
             def _():
-                base_send[slot, :, cols] = value.astype(jnp.bfloat16)
+                base_send[slot, here, cols] = value.astype(jnp.bfloat16)
 
         @pl.when(jnp.logical_not(takes_base))
         def _():
-            base_copy(slot).start()
-
-    def finish(slot):
-        code = codes(slot)
-        low_copy(slot).wait_recv()
-        low = low_own[slot] + low_recv[slot]
+            base_copy(slot, h).start()
+
+    def finish(slot, h):
+        here = span(h)
+        code = code_of[slot, here]
+        low_copy(slot, h).wait_recv()
+        low = low_own[slot, here] + low_recv[slot, here]
         spread = jnp.concatenate(
             [jnp.where(mask_of(code, j), low, 0.0).astype(jnp.bfloat16) for j in range(groups)],
             axis=1,
         )
-        gain = jnp.zeros((rows, 128), jnp.float32)
+        gain = jnp.zeros((half, 128), jnp.float32)
         for g in range(slots_per_owner):
             mine = code == (me * slots_per_owner + g + 0 * lane).astype(jnp.float32)
             gain = gain + jnp.where(mine, scale[g], 0.0)
@@ -271,56 +282,65 @@
         def _(n):
             cols = pl.ds(pl.multiple_of(n * TILE, TILE), TILE)
             value = jnp.dot(spread, up[:, cols], preferred_element_type=jnp.float32)
-            result[slot, :, cols] = (value * gain).astype(jnp.bfloat16)
+            result[slot, here, cols] = (value * gain).astype(jnp.bfloat16)
 
         @pl.when(takes_base)
         def _():
-            base_copy(slot).wait_recv()
+            base_copy(slot, h).wait_recv()
 
             @pl.loop(0, width // TILE)
             def _(n):
-                here = pl.ds(pl.multiple_of(n * TILE, TILE), TILE)
+                own = pl.ds(pl.multiple_of(n * TILE, TILE), TILE)
                 there = pl.ds(pl.multiple_of(column + n * TILE, TILE), TILE)
-                base = base_own[slot, :, here] + base_recv[slot, :, here].astype(jnp.float32)
-                result[slot, :, there] = (
-                    result[slot, :, there].astype(jnp.float32) + base
+                base = base_own[slot, here, own] + base_recv[slot, here, own].astype(jnp.float32)
+                result[slot, here, there] = (
+                    result[slot, here, there].astype(jnp.float32) + base
                 ).astype(jnp.bfloat16)
 
-    @pl.loop(0, 5)
+    def item(k):
+        slot = jnp.where(k < 2, 0, jnp.where(k < 6, 1 + k % 2, 3))
+        h = jnp.where(k < 2, k, jnp.where(k < 6, (k - 2) // 2, k - 6))
+        return jnp.where(first, k // HALVES, slot), jnp.where(first, k % HALVES, h)
+
+    total = 4 * HALVES
+    lag = jnp.where(first, 0, 2)
+
+    @pl.loop(0, total + 2)
     def _(step):
-        @pl.when(first & (step >= 1) & (step < 4))
-        def _():
-            for c in range(CHUNKS):
-                tok_copy(0, tok_hbm, step, c, v1).wait_recv()
-
-        @pl.when(second & (step == 1))
-        def _():
-            for c in range(CHUNKS):
-                tok_copy(0, tok_hbm, 1, c, v0).wait_recv()
-                tok_copy(2, tok.at[1], 3, c, v2).start()
-                tok_copy(0, tok_hbm, 2, c, v0).wait_recv()
-                tok_copy(3, tok.at[2], 2, c, v0).start()
-
-        @pl.when(second & (step == 3))
-        def _():
-            for c in range(CHUNKS):
-                tok_copy(0, tok_hbm, 3, c, v0).wait_recv()
-                tok_copy(4, tok.at[3], 3, c, v0).start()
-
-        @pl.when(step < 4)
-        def _():
-            project(step)
-
-        done = jnp.where(first, step, step - 1)
-
-        @pl.when((done >= 0) & (done < 4))
-        def _():
-            finish(done)
-
-        @pl.when(first & (done >= 1) & (done < 4))
-        def _():
-            for c in range(CHUNKS):
-                res_copy(done, done - 1, c, v1).start()
+        now = jnp.minimum(step, total - 1)
+        slot, h = item(now)
+
+        @pl.when(first & (step >= HALVES) & (step < total))
+        def _():
+            tok_copy(0, tok_hbm, slot, h, v1).wait_recv()
+
+        @pl.when(second & ((step == 2) | (step == 4)))
+        def _():
+            tok_copy(0, tok_hbm, 1, h, v0).wait_recv()
+            tok_copy(2, tok.at[1], 3, h, v2).start()
+            tok_copy(0, tok_hbm, 2, h, v0).wait_recv()
+            tok_copy(3, tok.at[2], 2, h, v0).start()
+
+        @pl.when(second & (step >= 6) & (step < total))
+        def _():
+            tok_copy(0, tok_hbm, 3, h, v0).wait_recv()
+            tok_copy(4, tok.at[3], 3, h, v0).start()
+
+        @pl.when(step < total)
+        def _():
+            project(slot, h)
+
+        late = jnp.clip(step - lag, 0, total - 1)
+        slot_done, h_done = item(late)
+
+        @pl.when((step >= lag) & (step < total + lag))
+        def _():
+            finish(slot_done, h_done)
+
+        @pl.when(first & (step >= HALVES) & (step < total))
+        def _():
+            for c in range(per_half):
+                res_copy(slot_done, slot_done - 1, h_done * per_half + c, v1).start()
 
     def add_arrived(slot, source, c):
         res_copy(slot, source, c, v0).wait_recv()
@@ -347,23 +367,26 @@
     for k in range(1, 4):
         meta_copy(k).wait_send()
     for slot in range(4):
-        low_copy(slot).wait_send()
+        for h in range(HALVES):
+            low_copy(slot, h).wait_send()
 
     @pl.when(jnp.logical_not(takes_base))
     def _():
         for slot in range(4):
-            base_copy(slot).wait_send()
-
+            for h in range(HALVES):
+                base_copy(slot, h).wait_send()
+
+    for h in range(HALVES):
+        tok_copy(0, tok_hbm, 1, h, v0).wait_send()
     for c in range(CHUNKS):
-        tok_copy(0, tok_hbm, 1, c, v0).wait_send()
         for slot in range(1, 4):
             res_copy(slot, 0, c, v0).wait_send()
 
     @pl.when(second)
     def _():
-        for c in range(CHUNKS):
+        for h in range(HALVES):
             for kind in range(1, 5):
-                tok_copy(kind, tok_hbm, 1, c, v0).wait_send()
+                tok_copy(kind, tok_hbm, 1, h, v0).wait_send()
 
 
 def fused_local(
@@ -405,20 +428,21 @@
             pltpu.VMEM((4, rows, width), f32),
             pltpu.VMEM((4, rows, 128), f32),
             pltpu.VMEM((4, rows, 128), f32),
+            pltpu.VMEM((4, rows, 128), f32),
             dma((4,)),
-            dma((5, CHUNKS)),
-            dma((4, CHUNKS)),
+            dma((5, HALVES)),
+            dma((4, HALVES)),
             dma((4, CHUNKS)),
             dma((5, CHUNKS)),
             dma((3,)),
             dma((4,)),
-            dma((4,)),
-            dma((4,)),
-            dma((4,)),
-            dma((4,)),
+            dma((4, HALVES)),
+            dma((4, HALVES)),
+            dma((4, HALVES)),
+            dma((4, HALVES)),
         ],
         compiler_params=pltpu.CompilerParams(
-            collective_id=0, has_side_effects=True, vmem_limit_bytes=48 * 2**20
+            collective_id=0, has_side_effects=True, vmem_limit_bytes=62 * 2**20
         ),
         cost_estimate=pl.CostEstimate(
             flops=8 * rows * features * (width + 2 * deep),

time: 96.2 us -> 88.9 us (0.924)
  Pallas kernels: 91 us -> 85.4 us
  local copies, waits for them, and re-layouts: 4.32 us -> 2.56 us
    pallas_call x1, Pallas kernels: 91 us -> 85.4 us  [fused_local(): pl.pallas_call(functools.partial(chain_kernel, adapters), out_shape=jax.S...]
    unnamed x7 -> x1, local copies, waits for them, and re-layouts: 4.32 us -> 1.97 us
where the time goes in v2:
time: 88.9 us; the launch traced here: 88.7 us
  Pallas kernels  85.4 us (96%)
  local copies, waits for them, and re-layouts  2.56 us (3%)
    pallas_call x1, Pallas kernels, fused_local(): pl.pallas_call(functools.partial(chain_kernel, adapters), out_shape=jax.S...  85.4 us
    unnamed x1, local copies, waits for them, and re-layouts  1.97 us

profile of v2, /device:TPU:0, one launch (start us, length us, event | category | flops | bytes accessed | tf_op | source)
XLA Modules:
  0.0 88.7 jit_solution(17113197517306594026)
XLA Ops:
  0.0 0.7 fusion
  0.7 0.6 broadcast_in_dim.2.meta_in
  1.3 85.4 %shard_map.73 = bf16[128,2560]{1,0:T(8,128)(2,1)} custom-call(f32[8,128]{1,0:T(8,128)} %broadcast_in_dim.2.meta_in, f32[8]{0:T(128)} %scale.1, bf16[128,2560]{1,0:T(8,128)(2,1)} %tok_hbm.1, bf16[2560,1280]{1,0:T(8,128)(2,1)} %w_hbm.1, bf16[512,2560]{1,0:T(8,128)(2,1)} %bitcast.8, bf16[512,2560]{1,0:T(8,128)(2,1)} %bitcast.9), custom_call_target="tpu_custom_call" | custom-call | flops 6039797760 | bytes 13107200 | tf_op jit(solution)/shard_map/pallas_call | solution.py:413
  86.7 2.0 %copy.9 = bf16[128,2560]{1,0:T(8,128)(2,1)} copy(bf16[128,2560]{1,0:T(8,128)(2,1)} %shard_map.73) | data formatting | bytes 1310720

commit v3 on v2

--- a/solution.py
+++ b/solution.py
@@ -10,7 +10,7 @@
 
 MESH = pl.DeviceIdType.MESH
 HALVES = 2
-CHUNKS = 8
+CHUNKS = 4
 TILE = 256
 
 
@@ -349,20 +349,33 @@
             + arrived[source, part(c)].astype(jnp.float32)
         ).astype(jnp.bfloat16)
 
-    @pl.when(second)
-    def _():
-        for slot, source, dst, target in ((2, 1, 3, v2), (3, 2, 4, v2), (1, 4, 0, v0)):
-            for c in range(CHUNKS):
-                add_arrived(slot, source, c)
-                res_copy(slot, dst, c, target).start()
-        for c in range(CHUNKS):
-            add_arrived(0, 3, c)
-
-    for c in range(CHUNKS):
+    def pass_on(slot, source, dst, c, target):
+        add_arrived(slot, source, c)
+        res_copy(slot, dst, c, target).start()
+
+    def deliver(c):
         res_copy(0, 0, c, v0).wait_recv()
         out_ref[part(c)] = (
             result[0, part(c)].astype(jnp.float32) + arrived[0, part(c)].astype(jnp.float32)
         ).astype(jnp.bfloat16)
+
+    @pl.when(second)
+    def _():
+        for c in range(CHUNKS):
+            pass_on(2, 1, 3, c, v2)
+        for c in range(CHUNKS + 1):
+            if c < CHUNKS:
+                pass_on(3, 2, 4, c, v2)
+            if c > 0:
+                pass_on(1, 4, 0, c - 1, v0)
+        for c in range(CHUNKS):
+            add_arrived(0, 3, c)
+            deliver(c)
+
+    @pl.when(first)
+    def _():
+        for c in range(CHUNKS):
+            deliver(c)
 
     for k in range(1, 4):
         meta_copy(k).wait_send()

time: 88.9 us -> 86.6 us (0.974)
  Pallas kernels: 85.4 us -> 83.2 us
    pallas_call x1, Pallas kernels: 85.4 us -> 83.2 us  [fused_local(): pl.pallas_call(functools.partial(chain_kernel, adapters), out_shape=jax.S...]
where the time goes in v3:
time: 86.6 us; the launch traced here: 86.4 us
  Pallas kernels  83.2 us (96%)
  local copies, waits for them, and re-layouts  2.56 us (3%)
    pallas_call x1, Pallas kernels, fused_local(): pl.pallas_call(functools.partial(chain_kernel, adapters), out_shape=jax.S...  83.2 us
    unnamed x1, local copies, waits for them, and re-layouts  1.97 us

profile of v3, /device:TPU:0, one launch (start us, length us, event | category | flops | bytes accessed | tf_op | source)
XLA Modules:
  0.0 86.4 jit_solution(14092404188209420281)
XLA Ops:
  0.0 0.7 fusion
  0.7 0.6 broadcast_in_dim.2.meta_in
  1.3 83.2 %shard_map.73 = bf16[128,2560]{1,0:T(8,128)(2,1)} custom-call(f32[8,128]{1,0:T(8,128)} %broadcast_in_dim.2.meta_in, f32[8]{0:T(128)} %scale.1, bf16[128,2560]{1,0:T(8,128)(2,1)} %tok_hbm.1, bf16[2560,1280]{1,0:T(8,128)(2,1)} %w_hbm.1, bf16[512,2560]{1,0:T(8,128)(2,1)} %bitcast.8, bf16[512,2560]{1,0:T(8,128)(2,1)} %bitcast.9), custom_call_target="tpu_custom_call" | custom-call | flops 6039797760 | bytes 13107200 | tf_op jit(solution)/shard_map/pallas_call | solution.py:426
  84.5 2.0 %copy.9 = bf16[128,2560]{1,0:T(8,128)(2,1)} copy(bf16[128,2560]{1,0:T(8,128)(2,1)} %shard_map.73) | data formatting | bytes 1310720

commit v4 on v3

--- a/solution.py
+++ b/solution.py
@@ -110,7 +110,7 @@
 
 def chain_kernel(
     slots_per_owner,
-    meta_in, scale, tok_hbm, w_hbm, down_hbm, up_hbm, out_ref,
+    meta_in, scale, tok_hbm, w_hbm, down_hbm, up_hbm, own_ref, last_ref,
     tok, w, down, up, meta, arrived, result, base_send, base_recv, base_own, low_own, low_recv, code_of,
     load_sem, tok_send, tok_recv, res_send, res_recv,
     meta_send, meta_recv, low_ssem, low_rsem, base_ssem, base_rsem,
@@ -355,9 +355,8 @@
 
     def deliver(c):
         res_copy(0, 0, c, v0).wait_recv()
-        out_ref[part(c)] = (
-            result[0, part(c)].astype(jnp.float32) + arrived[0, part(c)].astype(jnp.float32)
-        ).astype(jnp.bfloat16)
+        own_ref[part(c)] = result[0, part(c)]
+        last_ref[part(c)] = arrived[0, part(c)]
 
     @pl.when(second)
     def _():
@@ -423,11 +422,11 @@
     dma = pltpu.SemaphoreType.DMA
     vmem = pl.BlockSpec(memory_space=pltpu.VMEM)
     far = pl.BlockSpec(memory_space=pl.ANY)
-    return pl.pallas_call(
+    own, last = pl.pallas_call(
         functools.partial(chain_kernel, adapters),
-        out_shape=jax.ShapeDtypeStruct((rows, features), bf16),
+        out_shape=[jax.ShapeDtypeStruct((rows, features), bf16)] * 2,
         in_specs=[vmem, pl.BlockSpec(memory_space=pltpu.SMEM), far, far, far, far],
-        out_specs=vmem,
+        out_specs=[vmem, vmem],
         scratch_shapes=[
             pltpu.VMEM((4, rows, features), bf16),
             pltpu.VMEM((features, width), bf16),
@@ -463,6 +462,7 @@
             transcendentals=0,
         ),
     )(meta, adapter_output_scale, tokens, base_projection_weight, down, up)
+    return (own.astype(f32) + last.astype(f32)).astype(bf16)
 
 
 def fits(mesh):

time: 86.6 us -> 87.1 us (level)
  other arithmetic: 0.68 us -> 2.95 us
  local copies, waits for them, and re-layouts: 2.56 us -> 0.6 us
    convert_element_type x0 -> x1, other arithmetic: none -> 2.27 us  [fused_local(): return (own.astype(f32) + last.astype(f32)).astype(bf16)]
    unnamed x1 -> x0, local copies, waits for them, and re-layouts: 1.97 us -> none
where the time goes in v4:
time: 87.1 us; the launch traced here: 86.9 us
  Pallas kernels  83.4 us (96%)
  other arithmetic  2.95 us (3%)
    pallas_call x1, Pallas kernels, fused_local(): pl.pallas_call(functools.partial(chain_kernel, adapters), out_shape=[jax....  83.4 us
    convert_element_type x1, other arithmetic, fused_local(): return (own.astype(f32) + last.astype(f32)).astype(bf16)  2.27 us

profile of v4, /device:TPU:0, one launch (start us, length us, event | category | flops | bytes accessed | tf_op | source)
XLA Modules:
  0.0 86.9 jit_solution(11074157872168471181)
XLA Ops:
  0.0 0.7 fusion
  0.7 0.6 broadcast_in_dim.2.meta_in
  1.3 83.4 %shard_map.73 = (bf16[128,2560]{1,0:T(8,128)(2,1)}, bf16[128,2560]{1,0:T(8,128)(2,1)}) custom-call(f32[8,128]{1,0:T(8,128)} %broadcast_in_dim.2.meta_in, f32[8]{0:T(128)} %scale.1, bf16[128,2560]{1,0:T(8,128)(2,1)} %tok_hbm.1, bf16[2560,1280]{1,0:T(8,128)(2,1)} %w_hbm.1, bf16[512,2560]{1,0:T(8,128)(2,1)} %bitcast.8, bf16[512,2560]{1,0:T(8,128)(2,1)} %bitcast.9), custom_call_target="tpu_custom_call" | custom-call | flops 6039797760 | bytes 13107200 | tf_op jit(solution)/shard_map/pallas_call | solution.py:425
  84.7 2.3 %add_convert_fusion = bf16[128,2560]{1,0:T(8,128)(2,1)} fusion(bf16[128,2560]{1,0:T(8,128)(2,1)} %get-tuple-element.8, bf16[128,2560]{1,0:T(8,128)(2,1)} %get-tuple-element.7), kind=kLoop, calls=%fused_computation | loop fusion | flops 1310720 | bytes 1966080 | tf_op jit(solution)/shard_map/convert_element_type | solution.py:465
